TPU v7x, 512 devices: a whole 4x8x8 slice. The times are simulated.
512 devices in a mesh: dp: 32 (over y_hi, z, core), tensor: 16 (over x, y_lo).
Axes of the slice: x: 4, y: 8 (y_hi: 2, y_lo: 4; y = y_hi * 4 + y_lo), z: 8, core: 2. Of those that a mesh axis runs over, the one named last changes fastest.
Arguments:
- hidden_acts: bfloat16 [65536, 14336], P('dp', 'tensor'), may hold values from -6 to 6
- out_grads: bfloat16 [65536, 4096], P('dp', 'tensor'), may hold values from -6 to 6
- proj_in: bfloat16 [14336, 64], P('tensor'), may hold values from -0.046875 to 0.046875
- proj_out: bfloat16 [4096, 64], P('tensor'), may hold values from -0.09375 to 0.09375
- segments: int32 [32, 65536], P(None, 'dp'), may hold values from 0 to 1, as said below
- doc_counts: int32 [32], P('dp'), may hold values from 10 to 32
Outputs:
- doc_grads: bfloat16 [1024, 4096], P('dp', 'tensor')
- fisher: float32 [4096, 4096], P('dp', 'tensor')
Inputs may be any that keep to these rules, and one draw needn't show every extreme that they name: `segments`: every token belongs to exactly one slot of its shard; within one shard's 2048 tokens the slots 0 to 31 are contiguous runs in that order, each holding at least one token.
All inputs are finite; a program needn't handle non-finite values.
Results may differ from a plain program's by a relative error of at most 0.0062.
Values may be sent and summed in bfloat16 or wider, within the bound.
A program may use at most 64 MiB of HBM per device.

v0:
```python
import jax
import jax.numpy as jnp
from jax import lax
from jax.sharding import PartitionSpec as P

RANK = 64


def doc_sums_of(seg_live, dy_proj, x_proj):
    row_count = x_proj.shape[0]
    block_rows = 512
    summed = jnp.zeros((seg_live.shape[0], RANK * RANK), jnp.float32)
    for offset in range(0, row_count, block_rows):
        outer = (
            (
                dy_proj[offset : offset + block_rows, :, None]
                * x_proj[offset : offset + block_rows, None, :]
            )
            .reshape(block_rows, RANK * RANK)
            .astype(jnp.bfloat16)
        )
        summed = summed + jnp.dot(
            seg_live[:, offset : offset + block_rows], outer, preferred_element_type=jnp.float32
        )
    return summed


def transpose_product(left, right):
    return lax.dot_general(
        left, right, (((0,), (0,)), ((), ())), preferred_element_type=jnp.float32
    )


def per_device(hidden_acts, out_grads, proj_in, proj_out, segments, doc_counts):
    x_part = jnp.dot(hidden_acts, proj_in, preferred_element_type=jnp.float32)
    dy_part = jnp.dot(out_grads, proj_out, preferred_element_type=jnp.float32)
    partial_proj = jnp.concatenate([dy_part, x_part], axis=1)
    doc_total = segments.shape[0]
    live_docs = (jnp.arange(doc_total, dtype=jnp.int32) < doc_counts[0]).astype(jnp.int32)
    seg_int = segments * live_docs[:, None]
    seg_live = seg_int.astype(jnp.bfloat16)
    local_tokens = jnp.sum(seg_int).astype(jnp.float32)
    stacked = lax.psum(partial_proj, "tensor")
    doc_sums = doc_sums_of(seg_live, stacked[:, :RANK], stacked[:, RANK:])
    doc_grads = doc_sums.astype(jnp.bfloat16)
    col_width = doc_grads.shape[1] // lax.axis_size("tensor")
    col_block = lax.dynamic_slice_in_dim(
        doc_grads, lax.axis_index("tensor") * col_width, col_width, 1
    )
    total_tokens = lax.psum(local_tokens, "dp")
    fisher_block = lax.psum_scatter(
        transpose_product(doc_grads, col_block), "dp", scatter_dimension=0, tiled=True
    )
    return (col_block, fisher_block / total_tokens)


def solution(mesh):
    return jax.shard_map(
        per_device,
        mesh=mesh,
        in_specs=(
            P("dp", "tensor"),
            P("dp", "tensor"),
            P("tensor", None),
            P("tensor", None),
            P(None, "dp"),
            P("dp"),
        ),
        out_specs=(P("dp", "tensor"), P("dp", "tensor")),
        check_vma=False,
    )
```

profile of v0, /device:TPU:1, one launch (start us, length us, event | category | flops | bytes accessed | tf_op | source)
XLA Modules:
  0.0 359.6 jit_solution(8080208592829966887)
XLA Ops:
  7.2 0.0 copy-start
  7.2 0.0 all-reduce.2.cloned.1.call-start
  7.2 1.2 copy-done
  8.4 1.2 fusion.7
  9.6 0.0 copy-start.1
  9.6 3.3 fusion.8
  12.9 1.1 pad_maximum_fusion
  14.0 0.0 all-reduce.2.cloned.1.call-update
  14.0 0.0 reduce-scatter.2.cloned.1.call-start
  14.8 0.0 copy-done.1
  14.8 0.8 multiply_reduce_fusion
  15.5 165.1 %all-reduce.2.cloned.1.call-done = f32[2048,128]{0,1:T(8,128)} async-done(((f32[2048,128]{0,1:T(8,128)}), f32[2048,128]{0,1:T(8,128)}) %all-reduce.2.cloned.1.call-update) | async-done | bytes 1048592 | tf_op jit(solution)/shard_map/psum | solution.py:43
  180.6 1.4 fusion.6
  182.0 3.3 multiply_convert_fusion.2
  185.2 1.3 fusion.4
  186.5 1.3 convolution_add_fusion.2
  187.9 3.3 multiply_convert_fusion
  191.1 1.3 convolution_add_fusion.1
  192.5 1.3 fusion
  193.8 0.0 copy-start.2
  193.8 2.7 fusion.9
  196.5 0.0 reduce-scatter.2.cloned.1.call-update
  196.6 0.0 copy-done.2
  197.2 95.8 %psum.15 = f32[]{:T(128)} all-reduce(f32[]{:T(128)S(6)} %convert_element_type.51), channel_id=1, replica_groups=mesh['dp'=32,'tensor'=16] {'dp'}, use_global_device_ids=true, to_apply=%region_3.0 | all-reduce | flops 1 | bytes 8 | tf_op jit(solution)/shard_map/psum | solution.py:50
  293.0 57.6 %reduce-scatter.2.cloned.1.call-done = f32[128,256]{1,0:T(8,128)} async-done(((f32[4096,256]{1,0:T(8,128)}), f32[128,256]{1,0:T(8,128)}) %reduce-scatter.2.cloned.1.call-update) | async-done | bytes 131088 | tf_op jit(solution)/shard_map/reduce_scatter | solution.py:51
  350.6 2.1 broadcast_divide_fusion
  (2 shorter events, 0.0 us)
Async XLA Ops:
  7.2 1.2 copy-start
  7.2 173.4 %all-reduce.2.cloned.1.call-start = ((), (), s32[]{:S(2)}) async-start(), calls=%async_computation.1 | async-start | bytes 2097152 | tf_op jit(solution)/shard_map/psum | solution.py:43
  9.6 5.2 %copy-start.1 = (s32[32,2048]{1,0:T(8,128)S(1)}, s32[32,2048]{1,0:T(8,128)}, u32[]{:S(2)}) copy-start(s32[32,2048]{1,0:T(8,128)} %param.10) | copy-start | bytes 786436
  14.0 336.6 %reduce-scatter.2.cloned.1.call-start = ((), (), s32[]{:S(2)}) async-start(), calls=%async_computation.2 | async-start | bytes 4325376 | tf_op jit(solution)/shard_map/reduce_scatter | solution.py:51
  193.8 2.7 copy-start.2
Sparse Core Ops, SparseCore 0:
  14.2 166.3 all-reduce.1
  196.7 153.8 reduce-scatter.1
where the time goes:
time: 363 us; the launch traced here: 360 us
  waiting for transfers between devices  223 us (61%)
  blocking collectives  95.8 us (26%)
  between operations  15.4 us (4%)
  matrix products  12.5 us (3%)
  other arithmetic  10.5 us (3%)
    psum x1, waiting for transfers between devices, per_device(): stacked = lax.psum(partial_proj, 'tensor')  165 us
    psum x1, blocking collectives, per_device(): total_tokens = lax.psum(local_tokens, 'dp')  95.8 us
    reduce_scatter x1, waiting for transfers between devices, per_device(): lax.psum_scatter(transpose_product(doc_grads, col_block), 'dp', scatter_d...  57.6 us
  transfers between devices with their start and end apart: 2, of which 2 were waited for; matrix products, arithmetic and copies ran while one was open for 0% of the time, Pallas kernels for 0%

commit v1 on v0

v1 whole, which is shorter than its diff:
```python
import jax
import jax.numpy as jnp
from jax import lax
from jax.experimental import pallas as pl
from jax.experimental.pallas import tpu as pltpu
from jax.sharding import PartitionSpec as P

MESH = pl.DeviceIdType.MESH
F32 = jnp.float32
BF16 = jnp.bfloat16
RANK = 64
QUART = 16
CHUNKS = 4
DOCS = 32
COLS = 256
NT = (((1,), (1,)), ((), ()))
TN = (((0,), (0,)), ((), ()))


def dot(left, right, dims):
    return lax.dot_general(left, right, dims, preferred_element_type=F32)


def to_doc_rows(tile):
    turned = tile.astype(F32).T
    return jnp.concatenate([turned[DOCS * a : DOCS * (a + 1)] for a in range(4)], axis=1).astype(BF16)


def kernel(
    acts, grads, pin, pout, seg, counts, doc_out, fis_out,
    acts_v, grads_v, dy_part, x_part, x_send, dy_got, x_got, dy_send2, x_send2, dy_got2, x_got2,
    live_v, wide, sums, c_own, c_turn, g_col, g_row, f_part, f_got,
    in_sem, send_sem, recv_sem,
):
    i, j = lax.axis_index("dp"), lax.axis_index("tensor")
    k, c = i // 2, i % 2
    jx, jy = j // 4, j % 4
    x_peers = [(i, (jx + d) % 4 * 4 + jy) for d in (1, 2, 3)]
    y_peers = [(i, jx * 4 + (jy + d) % 4) for d in (1, 2, 3)]
    xy_peers = [(i, (j + d) % 16) for d in range(1, 16)]
    dp_peers = [((k + d) % 16 * 2 + c, j) for d in range(1, 16)]
    sibling = (2 * k + 1 - c, j)
    turn_to = [((jx * 4 + (jy + d) % 4) * 2 + c, k) for d in range(4)]
    turn_from = [(j * 2 + c, k // 4 * 4 + (k + d) % 4) for d in range(4)]
    on_diagonal = j == k

    rows = acts.shape[0] // CHUNKS
    loads = [pltpu.make_async_copy(grads, grads_v, in_sem.at[CHUNKS])]
    loads += [
        pltpu.make_async_copy(acts.at[pl.ds(n * rows, rows)], acts_v.at[pl.ds(n * rows, rows)], in_sem.at[n])
        for n in range(CHUNKS)
    ]
    for load in loads:
        load.start()

    barrier = pltpu.get_barrier_semaphore()

    def greet(peer):
        pl.semaphore_signal(barrier, inc=1, device_id=peer, device_id_type=MESH)

    for peer in xy_peers + dp_peers + [sibling] + turn_to[1:] + turn_from[1:]:
        greet(peer)

    @pl.when(jnp.logical_not(on_diagonal))
    def _():
        greet(turn_to[0])
        greet(turn_from[0])

    def remote(src, dst, sem, peer):
        return pltpu.make_async_remote_copy(
            src_ref=src, dst_ref=dst, send_sem=send_sem.at[sem], recv_sem=recv_sem.at[sem],
            device_id=peer, device_id_type=MESH,
        )

    def wait_for(buffer, sems, sem):
        pltpu.make_async_copy(buffer, buffer, sems.at[sem]).wait()

    pout_t = pout[...].astype(F32).T.astype(BF16)
    pin_t = pin[...].astype(F32).T.astype(BF16)
    loads[0].wait()
    for n in range(CHUNKS):
        part = pl.ds(n * rows, rows)
        dy_part[:, part] = dot(pout_t, grads_v[part, :], NT)

    pl.semaphore_wait(barrier, jnp.where(on_diagonal, 37, 39))

    def block(index):
        return pl.ds(pl.multiple_of(index * QUART, QUART), QUART)

    for d, peer in enumerate(x_peers):
        remote(dy_part.at[block((jx + d + 1) % 4)], dy_got.at[d], 0, peer).start()

    for n in range(CHUNKS):
        part = pl.ds(n * rows, rows)
        loads[n + 1].wait()
        product = dot(pin_t, acts_v[part, :], NT)
        x_part[:, part] = product
        x_send[:, part] = product.astype(BF16)
    for d, peer in enumerate(y_peers):
        remote(x_send.at[block((jy + d + 1) % 4)], x_got.at[d], 1, peer).start()

    live = jnp.where(lax.broadcasted_iota(jnp.int32, seg.shape, 0) < counts[0], seg[...], 0).astype(F32)
    live_v[...] = live
    tokens = jnp.sum(live)

    wait_for(dy_got, recv_sem, 0)
    dy_sum = dy_part[block(jx), :] + dy_got[0] + dy_got[1] + dy_got[2]
    dy_send2[...] = dy_sum.astype(BF16)
    for d, peer in enumerate(y_peers):
        remote(dy_send2, dy_got2.at[d], 2, peer).start()

    wait_for(x_got, recv_sem, 1)
    x_send2[...] = x_part[block(jy), :] + x_got[0].astype(F32) + x_got[1].astype(F32) + x_got[2].astype(F32)
    for d, peer in enumerate(x_peers):
        remote(x_send2, x_got2.at[d], 3, peer).start()

    wait_for(dy_got2, recv_sem, 2)
    dy_all = dy_sum + dy_got2[0].astype(F32) + dy_got2[1].astype(F32) + dy_got2[2].astype(F32)
    for a in range(QUART):
        wide[a * DOCS : (a + 1) * DOCS, :] = (live_v[...] * dy_all[a : a + 1, :]).astype(BF16)
    wait_for(x_got2, recv_sem, 3)
    x_all = x_send2[...] + x_got2[0] + x_got2[1] + x_got2[2]
    x_high = x_all.astype(BF16)
    x_low = (x_all - x_high.astype(F32)).astype(BF16)
    both = dot(jnp.concatenate([x_high, x_low], axis=0), wide[...], NT)
    total = (both[:QUART] + both[QUART:]).astype(BF16)
    for q in range(4):
        sums[q] = total[:, q * 128 : (q + 1) * 128]

    for d in (1, 2, 3):
        remote(sums.at[(jy + d) % 4], c_turn.at[jy], 5, turn_to[d]).start()

    @pl.when(jnp.logical_not(on_diagonal))
    def _():
        remote(sums.at[jy], c_turn.at[jy], 9, turn_to[0]).start()

    for d, peer in enumerate(y_peers):
        remote(sums.at[(jy + d + 1) % 4], c_own.at[jy], 4, peer).start()
    c_own[jy] = sums[jy]

    @pl.when(on_diagonal)
    def _():
        c_turn[jy] = sums[jy]

    wait_for(c_own.at[pl.ds(0, 3)], recv_sem, 4)
    own = to_doc_rows(c_own[...].reshape(RANK, 128))
    doc_out[...] = own
    high = jnp.floor(tokens * (1.0 / 256.0)) * 256.0
    corner = lax.broadcasted_iota(jnp.int32, (QUART, COLS), 0) * COLS + lax.broadcasted_iota(
        jnp.int32, (QUART, COLS), 1
    )
    tail = jnp.where(corner == 0, high, jnp.where(corner == 1, tokens - high, 0.0)).astype(BF16)
    g_col[k] = jnp.concatenate([own, tail], axis=0)
    for peer in dp_peers:
        remote(g_col.at[k], g_col.at[k], 6, peer).start()

    wait_for(c_turn.at[pl.ds(0, 3)], recv_sem, 5)

    @pl.when(jnp.logical_not(on_diagonal))
    def _():
        wait_for(c_turn.at[0], recv_sem, 9)

    g_row[j] = to_doc_rows(c_turn[...].reshape(RANK, 128))
    for peer in xy_peers:
        remote(g_row.at[j], g_row.at[j], 7, peer).start()

    wait_for(g_col.at[pl.ds(0, 15)], recv_sem, 6)
    columns = g_col[:, :DOCS, :].reshape(16 * DOCS, COLS)
    live_tokens = jnp.sum(g_col[:, DOCS:, :].astype(F32))
    wait_for(g_row.at[pl.ds(0, 15)], recv_sem, 7)
    product = dot(g_row[...].reshape(16 * DOCS, COLS), columns, TN)
    f_part[0, :128] = product[:128]
    f_part[1, :128] = product[128:]
    f_part[:, 128:] = jnp.full((2, 8, COLS), live_tokens, F32)
    swap = remote(f_part.at[1 - c], f_got, 8, sibling)
    swap.start()
    wait_for(f_got, recv_sem, 8)
    count = f_got[128:129, :] + live_tokens
    fis_out[...] = (f_part[c, :128] + f_got[:128]) / count

    for buffer, sem in (
        (dy_got, 0), (x_got, 1), (dy_got2, 2), (x_got2, 3), (c_own.at[pl.ds(0, 3)], 4),
        (c_turn.at[pl.ds(0, 3)], 5), (g_col.at[pl.ds(0, 15)], 6), (g_row.at[pl.ds(0, 15)], 7), (f_got, 8),
    ):
        wait_for(buffer, send_sem, sem)

    @pl.when(jnp.logical_not(on_diagonal))
    def _():
        wait_for(c_turn.at[0], send_sem, 9)


def per_device(acts, grads, pin, pout, seg, counts):
    tok, hidden = acts.shape
    width = grads.shape[1]
    vmem, any_, smem = (pl.BlockSpec(memory_space=m) for m in (pltpu.VMEM, pl.ANY, pltpu.SMEM))
    return pl.pallas_call(
        kernel,
        out_shape=(
            jax.ShapeDtypeStruct((DOCS, COLS), BF16),
            jax.ShapeDtypeStruct((128, COLS), F32),
        ),
        in_specs=[any_, any_, vmem, vmem, vmem, smem],
        out_specs=(vmem, vmem),
        scratch_shapes=[
            pltpu.VMEM((tok, hidden), BF16),
            pltpu.VMEM((tok, width), BF16),
            pltpu.VMEM((RANK, tok), F32),
            pltpu.VMEM((RANK, tok), F32),
            pltpu.VMEM((RANK, tok), BF16),
            pltpu.VMEM((3, QUART, tok), F32),
            pltpu.VMEM((3, QUART, tok), BF16),
            pltpu.VMEM((QUART, tok), BF16),
            pltpu.VMEM((QUART, tok), F32),
            pltpu.VMEM((3, QUART, tok), BF16),
            pltpu.VMEM((3, QUART, tok), F32),
            pltpu.VMEM((DOCS, tok), F32),
            pltpu.VMEM((QUART * DOCS, tok), BF16),
            pltpu.VMEM((4, QUART, 128), BF16),
            pltpu.VMEM((4, QUART, 128), BF16),
            pltpu.VMEM((4, QUART, 128), BF16),
            pltpu.VMEM((16, DOCS + QUART, COLS), BF16),
            pltpu.VMEM((16, DOCS, COLS), BF16),
            pltpu.VMEM((2, 136, COLS), F32),
            pltpu.VMEM((136, COLS), F32),
            pltpu.SemaphoreType.DMA((CHUNKS + 1,)),
            pltpu.SemaphoreType.DMA((10,)),
            pltpu.SemaphoreType.DMA((10,)),
        ],
        compiler_params=pltpu.CompilerParams(
            collective_id=0, has_side_effects=True, vmem_limit_bytes=40 * 1024 * 1024
        ),
        cost_estimate=pl.CostEstimate(flops=10**9, bytes_accessed=6 * 10**6, transcendentals=0),
        name="logra",
    )(acts, grads, pin, pout, seg, counts)


def solution(mesh):
    return jax.shard_map(
        per_device,
        mesh=mesh,
        in_specs=(
            P("dp", "tensor"),
            P("dp", "tensor"),
            P("tensor", None),
            P("tensor", None),
            P(None, "dp"),
            P("dp"),
        ),
        out_specs=(P("dp", "tensor"), P("dp", "tensor")),
        check_vma=False,
    )
```

time: 363 us -> 66.1 us (0.18)
  waiting for transfers between devices: 223 us -> 0 us
  blocking collectives: 95.8 us -> 0 us
  Pallas kernels: 0 us -> 57.1 us
  between operations: 15.4 us -> 1.31 us
  matrix products: 12.5 us -> 0 us
  other arithmetic: 10.5 us -> 0 us
  local copies, waits for them, and re-layouts: 2.56 us -> 7.41 us
    psum x1 -> x0, waiting for transfers between devices: 165 us -> none  [per_device(): stacked = lax.psum(partial_proj, 'tensor')]
    psum x1 -> x0, blocking collectives: 95.8 us -> none  [per_device(): total_tokens = lax.psum(local_tokens, 'dp')]
    reduce_scatter x1 -> x0, waiting for transfers between devices: 57.6 us -> none  [per_device(): lax.psum_scatter(transpose_product(doc_grads, col_block), 'dp', scatter_d...]
    pallas_call x0 -> x1, Pallas kernels: none -> 57.1 us  [per_device(): pl.pallas_call(kernel, out_shape=(jax.ShapeDtypeStruct((DOCS, COLS), BF16...]
    dot_general x7 -> x0, matrix products: 12.5 us -> none  [the longest x4 5.3 us: doc_sums_of(): jnp.dot(seg_live[:, offset:offset + block_rows], outer, preferred_element...]
    convert_element_type x3 -> x0, other arithmetic: 6.53 us -> none  [the longest x2 6.53 us: doc_sums_of(): outer = (dy_proj[offset:offset + block_rows, :, None] * x_proj[offset:off...]
    unnamed x6 -> x10, local copies, waits for them, and re-layouts: 1.19 us -> 7.41 us
  transfers between devices with their start and end apart: 2 -> 0, of which waited for: 2 -> 0; matrix products, arithmetic and copies ran while one was open for 0% -> 0% of each run, Pallas kernels for 0% -> 0%
where the time goes in v1:
time: 66.1 us; the launch traced here: 65.8 us
  Pallas kernels  57.1 us (86%)
  local copies, waits for them, and re-layouts  7.41 us (11%)
  between operations  1.31 us (2%)
    pallas_call x1, Pallas kernels, per_device(): pl.pallas_call(kernel, out_shape=(jax.ShapeDtypeStruct((DOCS, COLS), BF16...  57.1 us
    unnamed x10, local copies, waits for them, and re-layouts  7.41 us

profile of v1, /device:TPU:1, one launch (start us, length us, event | category | flops | bytes accessed | tf_op | source)
XLA Modules:
  0.0 65.8 jit_solution(1383218845159613105)
XLA Ops:
  1.3 0.9 %copy.9.pout = bf16[256,64]{1,0:T(8,128)(2,1)S(1)} copy(bf16[256,64]{0,1:T(8,128)(2,1)} %param.9) | data formatting | bytes 65536 | tf_op args[3]
  2.2 1.1 %copy.8.pin = bf16[896,64]{1,0:T(8,128)(2,1)S(1)} copy(bf16[896,64]{0,1:T(8,128)(2,1)} %param.8) | data formatting | bytes 229376 | tf_op args[2]
  3.2 0.0 copy-start
  3.2 2.0 %copy-done = bf16[2048,896]{1,0:T(8,128)(2,1)S(1)} copy-done((bf16[2048,896]{1,0:T(8,128)(2,1)S(1)}, bf16[2048,896]{1,0:T(8,128)(2,1)}, u32[]{:S(2)}) %copy-start) | copy-done | bytes 3670040
  5.3 0.0 copy-start.1
  5.3 1.2 %copy-done.1 = bf16[2048,256]{1,0:T(8,128)(2,1)S(1)} copy-done((bf16[2048,256]{1,0:T(8,128)(2,1)S(1)}, bf16[2048,256]{1,0:T(8,128)(2,1)}, u32[]{:S(2)}) %copy-start.1) | copy-done | bytes 1048600
  6.5 0.0 copy-start.2
  6.5 0.9 %copy-done.2 = s32[32,2048]{1,0:T(8,128)S(1)} copy-done((s32[32,2048]{1,0:T(8,128)S(1)}, s32[32,2048]{1,0:T(8,128)}, u32[]{:S(2)}) %copy-start.2) | copy-done | bytes 262168
  7.4 57.1 %logra.1 = (bf16[32,256]{1,0:T(8,128)(2,1)S(1)}, f32[128,256]{1,0:T(8,128)S(1)}) custom-call(bf16[2048,896]{1,0:T(8,128)(2,1)S(1)} %copy-done, bf16[2048,256]{1,0:T(8,128)(2,1)S(1)} %copy-done.1, bf16[896,64]{1,0:T(8,128)(2,1)S(1)} %copy.8.pin, bf16[256,64]{1,0:T(8,128)(2,1)S(1)} %copy.9.pout, s32[32,2048]{1,0:T(8,128)S(1)} %copy-done.2, s32[1]{0:T(128)S(6)} %copy.12.counts), custom_call_target="tpu_custom_call" | custom-call | flops 1000000000 | bytes 6000000 | tf_op jit(solution)/shard_map/logra/pallas_call | solution.py:196
  64.6 0.6 copy.13
  65.2 0.7 copy.14
Async XLA Ops:
  3.2 2.0 %copy-start = (bf16[2048,896]{1,0:T(8,128)(2,1)S(1)}, bf16[2048,896]{1,0:T(8,128)(2,1)}, u32[]{:S(2)}) copy-start(bf16[2048,896]{1,0:T(8,128)(2,1)} %acts.1) | copy-start | bytes 11010052
  5.3 1.2 %copy-start.1 = (bf16[2048,256]{1,0:T(8,128)(2,1)S(1)}, bf16[2048,256]{1,0:T(8,128)(2,1)}, u32[]{:S(2)}) copy-start(bf16[2048,256]{1,0:T(8,128)(2,1)} %grads.1) | copy-start | bytes 3145732
  6.5 0.9 %copy-start.2 = (s32[32,2048]{1,0:T(8,128)S(1)}, s32[32,2048]{1,0:T(8,128)}, u32[]{:S(2)}) copy-start(s32[32,2048]{1,0:T(8,128)} %seg.1) | copy-start | bytes 786436

commit v2 on v1

--- a/solution.py
+++ b/solution.py
@@ -28,7 +28,7 @@
 
 def kernel(
     acts, grads, pin, pout, seg, counts, doc_out, fis_out,
-    acts_v, grads_v, dy_part, x_part, x_send, dy_got, x_got, dy_send2, x_send2, dy_got2, x_got2,
+    acts_v, grads_v, pin_v, pout_v, seg_v, dy_part, x_part, x_send, dy_got, x_got, dy_send2, x_send2, dy_got2, x_got2,
     live_v, wide, sums, c_own, c_turn, g_col, g_row, f_part, f_got,
     in_sem, send_sem, recv_sem,
 ):
@@ -45,7 +45,10 @@
     on_diagonal = j == k
 
     rows = acts.shape[0] // CHUNKS
-    loads = [pltpu.make_async_copy(grads, grads_v, in_sem.at[CHUNKS])]
+    loads = [
+        pltpu.make_async_copy(src, dst, in_sem.at[CHUNKS + n])
+        for n, (src, dst) in enumerate(((pout, pout_v), (grads, grads_v), (pin, pin_v), (seg, seg_v)))
+    ]
     loads += [
         pltpu.make_async_copy(acts.at[pl.ds(n * rows, rows)], acts_v.at[pl.ds(n * rows, rows)], in_sem.at[n])
         for n in range(CHUNKS)
@@ -75,12 +78,11 @@
     def wait_for(buffer, sems, sem):
         pltpu.make_async_copy(buffer, buffer, sems.at[sem]).wait()
 
-    pout_t = pout[...].astype(F32).T.astype(BF16)
-    pin_t = pin[...].astype(F32).T.astype(BF16)
     loads[0].wait()
+    loads[1].wait()
     for n in range(CHUNKS):
         part = pl.ds(n * rows, rows)
-        dy_part[:, part] = dot(pout_t, grads_v[part, :], NT)
+        dy_part[:, part] = dot(pout_v[...], grads_v[part, :], NT)
 
     pl.semaphore_wait(barrier, jnp.where(on_diagonal, 37, 39))
 
@@ -90,16 +92,18 @@
     for d, peer in enumerate(x_peers):
         remote(dy_part.at[block((jx + d + 1) % 4)], dy_got.at[d], 0, peer).start()
 
+    loads[2].wait()
     for n in range(CHUNKS):
         part = pl.ds(n * rows, rows)
-        loads[n + 1].wait()
-        product = dot(pin_t, acts_v[part, :], NT)
+        loads[n + 4].wait()
+        product = dot(pin_v[...], acts_v[part, :], NT)
         x_part[:, part] = product
         x_send[:, part] = product.astype(BF16)
     for d, peer in enumerate(y_peers):
         remote(x_send.at[block((jy + d + 1) % 4)], x_got.at[d], 1, peer).start()
 
-    live = jnp.where(lax.broadcasted_iota(jnp.int32, seg.shape, 0) < counts[0], seg[...], 0).astype(F32)
+    loads[3].wait()
+    live = jnp.where(lax.broadcasted_iota(jnp.int32, seg.shape, 0) < counts[0], seg_v[...], 0).astype(F32)
     live_v[...] = live
     tokens = jnp.sum(live)
 
@@ -172,11 +176,9 @@
     f_part[0, :128] = product[:128]
     f_part[1, :128] = product[128:]
     f_part[:, 128:] = jnp.full((2, 8, COLS), live_tokens, F32)
-    swap = remote(f_part.at[1 - c], f_got, 8, sibling)
-    swap.start()
+    remote(f_part.at[1 - c], f_got, 8, sibling).start()
     wait_for(f_got, recv_sem, 8)
-    count = f_got[128:129, :] + live_tokens
-    fis_out[...] = (f_part[c, :128] + f_got[:128]) / count
+    fis_out[...] = (f_part[c, :128] + f_got[:128]) / (f_got[128:129, :] + live_tokens)
 
     for buffer, sem in (
         (dy_got, 0), (x_got, 1), (dy_got2, 2), (x_got2, 3), (c_own.at[pl.ds(0, 3)], 4),
@@ -192,18 +194,21 @@
 def per_device(acts, grads, pin, pout, seg, counts):
     tok, hidden = acts.shape
     width = grads.shape[1]
-    vmem, any_, smem = (pl.BlockSpec(memory_space=m) for m in (pltpu.VMEM, pl.ANY, pltpu.SMEM))
+    vmem, hbm, smem = (pl.BlockSpec(memory_space=m) for m in (pltpu.VMEM, pltpu.HBM, pltpu.SMEM))
     return pl.pallas_call(
         kernel,
         out_shape=(
             jax.ShapeDtypeStruct((DOCS, COLS), BF16),
             jax.ShapeDtypeStruct((128, COLS), F32),
         ),
-        in_specs=[any_, any_, vmem, vmem, vmem, smem],
+        in_specs=[hbm, hbm, hbm, hbm, hbm, smem],
         out_specs=(vmem, vmem),
         scratch_shapes=[
             pltpu.VMEM((tok, hidden), BF16),
             pltpu.VMEM((tok, width), BF16),
+            pltpu.VMEM((RANK, hidden), BF16),
+            pltpu.VMEM((RANK, width), BF16),
+            pltpu.VMEM((DOCS, tok), jnp.int32),
             pltpu.VMEM((RANK, tok), F32),
             pltpu.VMEM((RANK, tok), F32),
             pltpu.VMEM((RANK, tok), BF16),
@@ -222,16 +227,16 @@
             pltpu.VMEM((16, DOCS, COLS), BF16),
             pltpu.VMEM((2, 136, COLS), F32),
             pltpu.VMEM((136, COLS), F32),
-            pltpu.SemaphoreType.DMA((CHUNKS + 1,)),
+            pltpu.SemaphoreType.DMA((CHUNKS + 4,)),
             pltpu.SemaphoreType.DMA((10,)),
             pltpu.SemaphoreType.DMA((10,)),
         ],
         compiler_params=pltpu.CompilerParams(
-            collective_id=0, has_side_effects=True, vmem_limit_bytes=40 * 1024 * 1024
+            collective_id=0, has_side_effects=True, vmem_limit_bytes=61 * 1024 * 1024
         ),
         cost_estimate=pl.CostEstimate(flops=10**9, bytes_accessed=6 * 10**6, transcendentals=0),
         name="logra",
-    )(acts, grads, pin, pout, seg, counts)
+    )(acts, grads, pin.T, pout.T, seg, counts)
 
 
 def solution(mesh):

time: 66.1 us -> 61.1 us (0.924)
  local copies, waits for them, and re-layouts: 7.41 us -> 2.89 us
    unnamed x10 -> x2, local copies, waits for them, and re-layouts: 7.41 us -> 2.89 us
where the time goes in v2:
time: 61.1 us; the launch traced here: 60.9 us
  Pallas kernels  56.7 us (93%)
  local copies, waits for them, and re-layouts  2.89 us (5%)
  between operations  1.29 us (2%)
    pallas_call x1, Pallas kernels, per_device(): pl.pallas_call(kernel, out_shape=(jax.ShapeDtypeStruct((DOCS, COLS), BF16...  56.7 us
    unnamed x2, local copies, waits for them, and re-layouts  2.89 us

profile of v2, /device:TPU:1, one launch (start us, length us, event | category | flops | bytes accessed | tf_op | source)
XLA Modules:
  0.0 60.9 jit_solution(5899164102866108447)
XLA Ops:
  1.3 56.7 %logra.1 = (bf16[32,256]{1,0:T(8,128)(2,1)}, f32[128,256]{1,0:T(8,128)}) custom-call(bf16[2048,896]{1,0:T(8,128)(2,1)} %acts.1, bf16[2048,256]{1,0:T(8,128)(2,1)} %grads.1, bf16[64,896]{1,0:T(8,128)(2,1)} %bitcast.2, bf16[64,256]{1,0:T(8,128)(2,1)} %bitcast.3, s32[32,2048]{1,0:T(8,128)} %seg.1, s32[1]{0:T(128)S(6)} %copy.10.counts), custom_call_target="tpu_custom_call" | custom-call | flops 1000000000 | bytes 6000000 | tf_op jit(solution)/shard_map/logra/pallas_call | solution.py:198
  58.0 1.3 %copy.11 = bf16[32,256]{1,0:T(8,128)(2,1)} copy(bf16[32,256]{1,0:T(8,128)(2,1)} %get-tuple-element.4) | data formatting | bytes 32768
  59.3 1.6 %copy.12 = f32[128,256]{1,0:T(8,128)} copy(f32[128,256]{1,0:T(8,128)} %get-tuple-element.5) | data formatting | bytes 262144

commit v3 on v2

v3 whole, which is shorter than its diff:
```python
import jax
import jax.numpy as jnp
from jax import lax
from jax.experimental import pallas as pl
from jax.experimental.pallas import tpu as pltpu
from jax.sharding import PartitionSpec as P

MESH = pl.DeviceIdType.MESH
F32 = jnp.float32
BF16 = jnp.bfloat16
RANK = 64
QUART = 16
CHUNKS = 4
HALVES = 2
DOCS = 32
COLS = 256
NT = (((1,), (1,)), ((), ()))
TN = (((0,), (0,)), ((), ()))


def dot(left, right, dims):
    return lax.dot_general(left, right, dims, preferred_element_type=F32)


def to_doc_rows(tile):
    turned = tile.astype(F32).T
    return jnp.concatenate([turned[DOCS * a : DOCS * (a + 1)] for a in range(4)], axis=1).astype(BF16)


def kernel(
    acts, grads, pin, pout, seg, counts, doc_out, fis_out,
    acts_v, grads_v, pin_v, pout_v, seg_v, dy_part, x_part, x_send, dy_got, x_got, dy_send2, x_send2, dy_got2, x_got2, dy_all,
    live_v, wide, sums, c_own, c_turn, g_col, g_row, f_part, f_got,
    in_sem, send_sem, recv_sem,
):
    i, j = lax.axis_index("dp"), lax.axis_index("tensor")
    k, c = i // 2, i % 2
    jx, jy = j // 4, j % 4
    x_peers = [(i, (jx + d) % 4 * 4 + jy) for d in (1, 2, 3)]
    y_peers = [(i, jx * 4 + (jy + d) % 4) for d in (1, 2, 3)]
    xy_peers = [(i, (jx + d) % 4 * 4 + (jy + e) % 4) for d in (2, 1, 3, 0) for e in (2, 1, 3, 0) if d or e]
    dp_peers = [
        (((k // 8 + e) % 2 * 8 + (k + d) % 8) * 2 + c, j)
        for e in (1, 0) for d in (4, 3, 5, 2, 6, 1, 7, 0) if d or e
    ]
    sibling = (2 * k + 1 - c, j)
    turn_to = [((jx * 4 + (jy + d) % 4) * 2 + c, k) for d in range(4)]
    turn_from = [(j * 2 + c, k // 4 * 4 + (k + d) % 4) for d in range(4)]
    on_diagonal = j == k

    rows = acts.shape[0] // CHUNKS
    span = acts.shape[0] // HALVES

    def load(src, dst, n):
        copy = pltpu.make_async_copy(src, dst, in_sem.at[n])
        copy.start()
        return copy

    pout_load, pin_load = load(pout, pout_v, 0), load(pin, pin_v, 1)
    grads_load, acts_load = [], []
    for h in range(HALVES):
        part = pl.ds(h * span, span)
        grads_load.append(load(grads.at[part], grads_v.at[part], 3 + h))
        for n in range(h * CHUNKS // HALVES, (h + 1) * CHUNKS // HALVES):
            part = pl.ds(n * rows, rows)
            acts_load.append(load(acts.at[part], acts_v.at[part], 3 + HALVES + n))
    seg_load = load(seg, seg_v, 2)

    barrier = pltpu.get_barrier_semaphore()

    def greet(peer):
        pl.semaphore_signal(barrier, inc=1, device_id=peer, device_id_type=MESH)

    for peer in xy_peers + dp_peers + [sibling] + turn_to[1:] + turn_from[1:]:
        greet(peer)

    @pl.when(jnp.logical_not(on_diagonal))
    def _():
        greet(turn_to[0])
        greet(turn_from[0])

    def remote(src, dst, sem, peer):
        return pltpu.make_async_remote_copy(
            src_ref=src, dst_ref=dst, send_sem=send_sem.at[sem], recv_sem=recv_sem.at[sem],
            device_id=peer, device_id_type=MESH,
        )

    def wait_for(buffer, sems, sem):
        pltpu.make_async_copy(buffer, buffer, sems.at[sem]).wait()

    def project(h):
        grads_load[h].wait()
        for n in range(CHUNKS // HALVES):
            part = pl.ds(n * rows, rows)
            dy_part[h, :, part] = dot(pout_v[...], grads_v[pl.ds(h * span + n * rows, rows), :], NT)
        for n in range(CHUNKS // HALVES):
            part = pl.ds(n * rows, rows)
            acts_load[h * CHUNKS // HALVES + n].wait()
            product = dot(pin_v[...], acts_v[pl.ds(h * span + n * rows, rows), :], NT)
            x_part[h, :, part] = product
            x_send[h, :, part] = product.astype(BF16)

    def block(index):
        return pl.ds(pl.multiple_of(index * QUART, QUART), QUART)

    def send_parts(h):
        for d, peer in enumerate(y_peers):
            remote(x_send.at[h, block((jy + d + 1) % 4)], x_got.at[h, d], 10 + h, peer).start()
        for d, peer in enumerate(x_peers):
            remote(dy_part.at[h, block((jx + d + 1) % 4)], dy_got.at[h, d], 12 + h, peer).start()

    pout_load.wait()
    pin_load.wait()
    project(0)
    pl.semaphore_wait(barrier, jnp.where(on_diagonal, 37, 39))
    send_parts(0)
    for h in range(1, HALVES):
        project(h)
        send_parts(h)

    seg_load.wait()
    live = jnp.where(lax.broadcasted_iota(jnp.int32, seg.shape, 0) < counts[0], seg_v[...], 0).astype(F32)
    live_v[...] = live
    tokens = jnp.sum(live)

    for h in range(HALVES):
        wait_for(dy_got.at[h], recv_sem, 12 + h)
        dy_sum = dy_part[h, block(jx), :] + dy_got[h, 0] + dy_got[h, 1] + dy_got[h, 2]
        dy_all[h] = dy_sum
        dy_send2[h] = dy_sum.astype(BF16)
        for d, peer in enumerate(y_peers):
            remote(dy_send2.at[h], dy_got2.at[h, d], 14 + h, peer).start()
        wait_for(x_got.at[h], recv_sem, 10 + h)
        got = [x_got[h, d].astype(F32) for d in range(3)]
        x_send2[h] = x_part[h, block(jy), :] + got[0] + got[1] + got[2]
        for d, peer in enumerate(x_peers):
            remote(x_send2.at[h], x_got2.at[h, d], 16 + h, peer).start()

    both = jnp.zeros((2 * QUART, QUART * DOCS), F32)
    for h in range(HALVES):
        wait_for(dy_got2.at[h], recv_sem, 14 + h)
        got = [dy_got2[h, d].astype(F32) for d in range(3)]
        dy_full = dy_all[h] + got[0] + got[1] + got[2]
        mask = live_v[:, h * span : (h + 1) * span]
        for a in range(QUART):
            wide[a * DOCS : (a + 1) * DOCS, :] = (mask * dy_full[a : a + 1, :]).astype(BF16)
        wait_for(x_got2.at[h], recv_sem, 16 + h)
        x_full = x_send2[h] + x_got2[h, 0] + x_got2[h, 1] + x_got2[h, 2]
        x_high = x_full.astype(BF16)
        x_low = (x_full - x_high.astype(F32)).astype(BF16)
        both = both + dot(jnp.concatenate([x_high, x_low], axis=0), wide[...], NT)
    total = (both[:QUART] + both[QUART:]).astype(BF16)
    for q in range(4):
        sums[q] = total[:, q * 128 : (q + 1) * 128]

    for d in (1, 2, 3):
        remote(sums.at[(jy + d) % 4], c_turn.at[jy], 5, turn_to[d]).start()

    @pl.when(jnp.logical_not(on_diagonal))
    def _():
        remote(sums.at[jy], c_turn.at[jy], 9, turn_to[0]).start()

    for d, peer in enumerate(y_peers):
        remote(sums.at[(jy + d + 1) % 4], c_own.at[jy], 4, peer).start()
    c_own[jy] = sums[jy]

    @pl.when(on_diagonal)
    def _():
        c_turn[jy] = sums[jy]

    wait_for(c_own.at[pl.ds(0, 3)], recv_sem, 4)
    own = to_doc_rows(c_own[...].reshape(RANK, 128))
    doc_out[...] = own
    high = jnp.floor(tokens * (1.0 / 256.0)) * 256.0
    corner = lax.broadcasted_iota(jnp.int32, (QUART, COLS), 0) * COLS + lax.broadcasted_iota(
        jnp.int32, (QUART, COLS), 1
    )
    tail = jnp.where(corner == 0, high, jnp.where(corner == 1, tokens - high, 0.0)).astype(BF16)
    g_col[k] = jnp.concatenate([own, tail], axis=0)
    for peer in dp_peers:
        remote(g_col.at[k], g_col.at[k], 6, peer).start()

    wait_for(c_turn.at[pl.ds(0, 3)], recv_sem, 5)

    @pl.when(jnp.logical_not(on_diagonal))
    def _():
        wait_for(c_turn.at[0], recv_sem, 9)

    g_row[j] = to_doc_rows(c_turn[...].reshape(RANK, 128))
    for peer in xy_peers:
        remote(g_row.at[j], g_row.at[j], 7, peer).start()

    wait_for(g_col.at[pl.ds(0, 15)], recv_sem, 6)
    columns = g_col[:, :DOCS, :].reshape(16 * DOCS, COLS)
    live_tokens = jnp.sum(g_col[:, DOCS:, :].astype(F32))
    wait_for(g_row.at[pl.ds(0, 15)], recv_sem, 7)
    product = dot(g_row[...].reshape(16 * DOCS, COLS), columns, TN)
    f_part[0, :128] = product[:128]
    f_part[1, :128] = product[128:]
    f_part[:, 128:] = jnp.full((2, 8, COLS), live_tokens, F32)
    remote(f_part.at[1 - c], f_got, 8, sibling).start()
    wait_for(f_got, recv_sem, 8)
    fis_out[...] = (f_part[c, :128] + f_got[:128]) / (f_got[128:129, :] + live_tokens)

    for h in range(HALVES):
        for buffer, sem in ((x_got, 10), (dy_got, 12), (dy_got2, 14), (x_got2, 16)):
            wait_for(buffer.at[h], send_sem, sem + h)
    for buffer, sem in (
        (c_own.at[pl.ds(0, 3)], 4), (c_turn.at[pl.ds(0, 3)], 5), (g_col.at[pl.ds(0, 15)], 6),
        (g_row.at[pl.ds(0, 15)], 7), (f_got, 8),
    ):
        wait_for(buffer, send_sem, sem)

    @pl.when(jnp.logical_not(on_diagonal))
    def _():
        wait_for(c_turn.at[0], send_sem, 9)


def hand_over(doc_in, fis_in, doc_out, fis_out):
    doc_out[...] = doc_in[...]
    fis_out[...] = fis_in[...]


def per_device(acts, grads, pin, pout, seg, counts):
    tok, hidden = acts.shape
    width, span = grads.shape[1], tok // HALVES
    vmem, hbm, smem = (pl.BlockSpec(memory_space=m) for m in (pltpu.VMEM, pltpu.HBM, pltpu.SMEM))
    shapes = (jax.ShapeDtypeStruct((DOCS, COLS), BF16), jax.ShapeDtypeStruct((128, COLS), F32))
    results = pl.pallas_call(
        kernel,
        out_shape=shapes,
        in_specs=[hbm, hbm, hbm, hbm, hbm, smem],
        out_specs=(vmem, vmem),
        scratch_shapes=[
            pltpu.VMEM((tok, hidden), BF16),
            pltpu.VMEM((tok, width), BF16),
            pltpu.VMEM((RANK, hidden), BF16),
            pltpu.VMEM((RANK, width), BF16),
            pltpu.VMEM((DOCS, tok), jnp.int32),
            pltpu.VMEM((HALVES, RANK, span), F32),
            pltpu.VMEM((HALVES, RANK, span), F32),
            pltpu.VMEM((HALVES, RANK, span), BF16),
            pltpu.VMEM((HALVES, 3, QUART, span), F32),
            pltpu.VMEM((HALVES, 3, QUART, span), BF16),
            pltpu.VMEM((HALVES, QUART, span), BF16),
            pltpu.VMEM((HALVES, QUART, span), F32),
            pltpu.VMEM((HALVES, 3, QUART, span), BF16),
            pltpu.VMEM((HALVES, 3, QUART, span), F32),
            pltpu.VMEM((HALVES, QUART, span), F32),
            pltpu.VMEM((DOCS, tok), F32),
            pltpu.VMEM((QUART * DOCS, span), BF16),
            pltpu.VMEM((4, QUART, 128), BF16),
            pltpu.VMEM((4, QUART, 128), BF16),
            pltpu.VMEM((4, QUART, 128), BF16),
            pltpu.VMEM((16, DOCS + QUART, COLS), BF16),
            pltpu.VMEM((16, DOCS, COLS), BF16),
            pltpu.VMEM((2, 136, COLS), F32),
            pltpu.VMEM((136, COLS), F32),
            pltpu.SemaphoreType.DMA((3 + HALVES + CHUNKS,)),
            pltpu.SemaphoreType.DMA((18,)),
            pltpu.SemaphoreType.DMA((18,)),
        ],
        compiler_params=pltpu.CompilerParams(
            collective_id=0, has_side_effects=True, vmem_limit_bytes=61 * 1024 * 1024
        ),
        cost_estimate=pl.CostEstimate(flops=10**9, bytes_accessed=6 * 10**6, transcendentals=0),
        name="logra",
    )(acts, grads, pin.T, pout.T, seg, counts)
    return pl.pallas_call(
        hand_over,
        out_shape=shapes,
        in_specs=[vmem, vmem],
        out_specs=(vmem, vmem),
        compiler_params=pltpu.CompilerParams(vmem_limit_bytes=61 * 1024 * 1024),
        name="hand_over",
    )(*results)


def solution(mesh):
    return jax.shard_map(
        per_device,
        mesh=mesh,
        in_specs=(
            P("dp", "tensor"),
            P("dp", "tensor"),
            P("tensor", None),
            P("tensor", None),
            P(None, "dp"),
            P("dp"),
        ),
        out_specs=(P("dp", "tensor"), P("dp", "tensor")),
        check_vma=False,
    )
```

time: 61.1 us -> 55.9 us (0.915)
  local copies, waits for them, and re-layouts: 2.89 us -> 0 us
  Pallas kernels: 56.7 us -> 54.4 us
    unnamed x2 -> x0, local copies, waits for them, and re-layouts: 2.89 us -> none
    pallas_call x1 -> x2, Pallas kernels: 56.7 us -> 54.4 us  [the longest x1 52.8 us: per_device(): pl.pallas_call(kernel, out_shape=shapes, in_specs=[hbm, hbm, hbm, hbm, hb...]
where the time goes in v3:
time: 55.9 us; the launch traced here: 55.6 us
  Pallas kernels  54.4 us (97%)
  between operations  1.29 us (2%)
    pallas_call x1, Pallas kernels, per_device(): pl.pallas_call(kernel, out_shape=shapes, in_specs=[hbm, hbm, hbm, hbm, hb...  52.8 us
    pallas_call x1, Pallas kernels, per_device(): pl.pallas_call(hand_over, out_shape=shapes, in_specs=[vmem, vmem], out_sp...  1.59 us

profile of v3, /device:TPU:1, one launch (start us, length us, event | category | flops | bytes accessed | tf_op | source)
XLA Modules:
  0.0 55.6 jit_solution(17320570690280330606)
XLA Ops:
  1.3 52.8 %logra.1 = (bf16[32,256]{1,0:T(8,128)(2,1)}, f32[128,256]{1,0:T(8,128)}) custom-call(bf16[2048,896]{1,0:T(8,128)(2,1)} %acts.1, bf16[2048,256]{1,0:T(8,128)(2,1)} %grads.1, bf16[64,896]{1,0:T(8,128)(2,1)} %bitcast.2, bf16[64,256]{1,0:T(8,128)(2,1)} %bitcast.3, s32[32,2048]{1,0:T(8,128)} %seg.1, s32[1]{0:T(128)S(6)} %copy.8.counts), custom_call_target="tpu_custom_call" | custom-call | flops 1000000000 | bytes 6000000 | tf_op jit(solution)/shard_map/logra/pallas_call | solution.py:229
  54.1 1.6 %hand_over.1 = (bf16[32,256]{1,0:T(8,128)(2,1)}, f32[128,256]{1,0:T(8,128)}) custom-call(bf16[32,256]{1,0:T(8,128)(2,1)} %get-tuple-element.4.doc_in, f32[128,256]{1,0:T(8,128)} %get-tuple-element.5.fis_in), custom_call_target="tpu_custom_call" | custom-call | tf_op jit(solution)/shard_map/hand_over/pallas_call | solution.py:269

commit v4 on v3

--- a/solution.py
+++ b/solution.py
@@ -30,7 +30,7 @@
 def kernel(
     acts, grads, pin, pout, seg, counts, doc_out, fis_out,
     acts_v, grads_v, pin_v, pout_v, seg_v, dy_part, x_part, x_send, dy_got, x_got, dy_send2, x_send2, dy_got2, x_got2, dy_all,
-    live_v, wide, sums, c_own, c_turn, g_col, g_row, f_part, f_got,
+    live_v, wide, sums, c_own, c_turn, g_col, g_row, f_send, f_got, count_own, count_got, count_all,
     in_sem, send_sem, recv_sem,
 ):
     i, j = lax.axis_index("dp"), lax.axis_index("tensor")
@@ -39,10 +39,10 @@
     x_peers = [(i, (jx + d) % 4 * 4 + jy) for d in (1, 2, 3)]
     y_peers = [(i, jx * 4 + (jy + d) % 4) for d in (1, 2, 3)]
     xy_peers = [(i, (jx + d) % 4 * 4 + (jy + e) % 4) for d in (2, 1, 3, 0) for e in (2, 1, 3, 0) if d or e]
-    dp_peers = [
-        (((k // 8 + e) % 2 * 8 + (k + d) % 8) * 2 + c, j)
-        for e in (1, 0) for d in (4, 3, 5, 2, 6, 1, 7, 0) if d or e
-    ]
+    y_hi, z = k // 8, k % 8
+    partner = ((k + 8) % 16) * 2 + c
+    across = [(partner, jx * 4 + (jy + d) % 4) for d in range(4)]
+    z_peers = [((y_hi * 8 + (z + d) % 8) * 2 + c, j) for d in (4, 3, 5, 2, 6, 1, 7)]
     sibling = (2 * k + 1 - c, j)
     turn_to = [((jx * 4 + (jy + d) % 4) * 2 + c, k) for d in range(4)]
     turn_from = [(j * 2 + c, k // 4 * 4 + (k + d) % 4) for d in range(4)]
@@ -56,14 +56,14 @@
         copy.start()
         return copy
 
-    pout_load, pin_load = load(pout, pout_v, 0), load(pin, pin_v, 1)
+    pin_load, pout_load = load(pin, pin_v, 1), load(pout, pout_v, 0)
     grads_load, acts_load = [], []
     for h in range(HALVES):
-        part = pl.ds(h * span, span)
-        grads_load.append(load(grads.at[part], grads_v.at[part], 3 + h))
         for n in range(h * CHUNKS // HALVES, (h + 1) * CHUNKS // HALVES):
             part = pl.ds(n * rows, rows)
             acts_load.append(load(acts.at[part], acts_v.at[part], 3 + HALVES + n))
+        part = pl.ds(h * span, span)
+        grads_load.append(load(grads.at[part], grads_v.at[part], 3 + h))
     seg_load = load(seg, seg_v, 2)
 
     barrier = pltpu.get_barrier_semaphore()
@@ -71,7 +71,7 @@
     def greet(peer):
         pl.semaphore_signal(barrier, inc=1, device_id=peer, device_id_type=MESH)
 
-    for peer in xy_peers + dp_peers + [sibling] + turn_to[1:] + turn_from[1:]:
+    for peer in xy_peers + z_peers + across + [sibling] + turn_to[1:] + turn_from[1:]:
         greet(peer)
 
     @pl.when(jnp.logical_not(on_diagonal))
@@ -89,16 +89,16 @@
         pltpu.make_async_copy(buffer, buffer, sems.at[sem]).wait()
 
     def project(h):
-        grads_load[h].wait()
-        for n in range(CHUNKS // HALVES):
-            part = pl.ds(n * rows, rows)
-            dy_part[h, :, part] = dot(pout_v[...], grads_v[pl.ds(h * span + n * rows, rows), :], NT)
         for n in range(CHUNKS // HALVES):
             part = pl.ds(n * rows, rows)
             acts_load[h * CHUNKS // HALVES + n].wait()
             product = dot(pin_v[...], acts_v[pl.ds(h * span + n * rows, rows), :], NT)
             x_part[h, :, part] = product
             x_send[h, :, part] = product.astype(BF16)
+        grads_load[h].wait()
+        for n in range(CHUNKS // HALVES):
+            part = pl.ds(n * rows, rows)
+            dy_part[h, :, part] = dot(pout_v[...], grads_v[pl.ds(h * span + n * rows, rows), :], NT)
 
     def block(index):
         return pl.ds(pl.multiple_of(index * QUART, QUART), QUART)
@@ -112,7 +112,7 @@
     pout_load.wait()
     pin_load.wait()
     project(0)
-    pl.semaphore_wait(barrier, jnp.where(on_diagonal, 37, 39))
+    pl.semaphore_wait(barrier, jnp.where(on_diagonal, 33, 35))
     send_parts(0)
     for h in range(1, HALVES):
         project(h)
@@ -121,7 +121,8 @@
     seg_load.wait()
     live = jnp.where(lax.broadcasted_iota(jnp.int32, seg.shape, 0) < counts[0], seg_v[...], 0).astype(F32)
     live_v[...] = live
-    tokens = jnp.sum(live)
+    count_own[...] = jnp.full(count_own.shape, jnp.sum(live), F32)
+    remote(count_own, count_got, 19, across[0]).start()
 
     for h in range(HALVES):
         wait_for(dy_got.at[h], recv_sem, 12 + h)
@@ -135,6 +136,11 @@
         x_send2[h] = x_part[h, block(jy), :] + got[0] + got[1] + got[2]
         for d, peer in enumerate(x_peers):
             remote(x_send2.at[h], x_got2.at[h, d], 16 + h, peer).start()
+
+    wait_for(count_got, recv_sem, 19)
+    count_all[z] = count_own[...] + count_got[...]
+    for peer in z_peers:
+        remote(count_all.at[z], count_all.at[z], 20, peer).start()
 
     both = jnp.zeros((2 * QUART, QUART * DOCS), F32)
     for h in range(HALVES):
@@ -160,25 +166,24 @@
     def _():
         remote(sums.at[jy], c_turn.at[jy], 9, turn_to[0]).start()
 
+    for d, peer in enumerate(across):
+        remote(sums.at[(jy + d) % 4], c_own.at[1, jy], 18, peer).start()
     for d, peer in enumerate(y_peers):
-        remote(sums.at[(jy + d + 1) % 4], c_own.at[jy], 4, peer).start()
-    c_own[jy] = sums[jy]
+        remote(sums.at[(jy + d + 1) % 4], c_own.at[0, jy], 4, peer).start()
+    c_own[0, jy] = sums[jy]
 
     @pl.when(on_diagonal)
     def _():
         c_turn[jy] = sums[jy]
 
-    wait_for(c_own.at[pl.ds(0, 3)], recv_sem, 4)
-    own = to_doc_rows(c_own[...].reshape(RANK, 128))
+    wait_for(c_own.at[0, pl.ds(0, 3)], recv_sem, 4)
+    own = to_doc_rows(c_own[0].reshape(RANK, 128))
     doc_out[...] = own
-    high = jnp.floor(tokens * (1.0 / 256.0)) * 256.0
-    corner = lax.broadcasted_iota(jnp.int32, (QUART, COLS), 0) * COLS + lax.broadcasted_iota(
-        jnp.int32, (QUART, COLS), 1
-    )
-    tail = jnp.where(corner == 0, high, jnp.where(corner == 1, tokens - high, 0.0)).astype(BF16)
-    g_col[k] = jnp.concatenate([own, tail], axis=0)
-    for peer in dp_peers:
-        remote(g_col.at[k], g_col.at[k], 6, peer).start()
+    g_col[z, y_hi] = own
+    wait_for(c_own.at[1], recv_sem, 18)
+    g_col[z, 1 - y_hi] = to_doc_rows(c_own[1].reshape(RANK, 128))
+    for peer in z_peers:
+        remote(g_col.at[z], g_col.at[z], 6, peer).start()
 
     wait_for(c_turn.at[pl.ds(0, 3)], recv_sem, 5)
 
@@ -186,28 +191,34 @@
     def _():
         wait_for(c_turn.at[0], recv_sem, 9)
 
-    g_row[j] = to_doc_rows(c_turn[...].reshape(RANK, 128))
+    slot = j % 8 * 2 + j // 8
+    g_row[slot] = to_doc_rows(c_turn[...].reshape(RANK, 128))
     for peer in xy_peers:
-        remote(g_row.at[j], g_row.at[j], 7, peer).start()
-
-    wait_for(g_col.at[pl.ds(0, 15)], recv_sem, 6)
-    columns = g_col[:, :DOCS, :].reshape(16 * DOCS, COLS)
-    live_tokens = jnp.sum(g_col[:, DOCS:, :].astype(F32))
+        remote(g_row.at[slot], g_row.at[slot], 7, peer).start()
+
+    wait_for(count_all.at[pl.ds(0, 7)], recv_sem, 20)
+    live_tokens = jnp.sum(count_all[:, 0, 0:1])
+    wait_for(g_col.at[pl.ds(0, 7)], recv_sem, 6)
+    columns = g_col[...].reshape(16 * DOCS, COLS)
     wait_for(g_row.at[pl.ds(0, 15)], recv_sem, 7)
-    product = dot(g_row[...].reshape(16 * DOCS, COLS), columns, TN)
-    f_part[0, :128] = product[:128]
-    f_part[1, :128] = product[128:]
-    f_part[:, 128:] = jnp.full((2, 8, COLS), live_tokens, F32)
-    remote(f_part.at[1 - c], f_got, 8, sibling).start()
+
+    def fisher_rows(half):
+        left = g_row[:, :, pl.ds(pl.multiple_of(half * 128, 128), 128)].reshape(16 * DOCS, 128)
+        return dot(left, columns, TN)
+
+    f_send[:128] = fisher_rows(1 - c)
+    f_send[128:] = jnp.full((8, COLS), live_tokens, F32)
+    remote(f_send, f_got, 8, sibling).start()
+    mine = fisher_rows(c)
     wait_for(f_got, recv_sem, 8)
-    fis_out[...] = (f_part[c, :128] + f_got[:128]) / (f_got[128:129, :] + live_tokens)
+    fis_out[...] = (mine + f_got[:128]) / (f_got[128:129, :] + live_tokens)
 
     for h in range(HALVES):
         for buffer, sem in ((x_got, 10), (dy_got, 12), (dy_got2, 14), (x_got2, 16)):
             wait_for(buffer.at[h], send_sem, sem + h)
     for buffer, sem in (
-        (c_own.at[pl.ds(0, 3)], 4), (c_turn.at[pl.ds(0, 3)], 5), (g_col.at[pl.ds(0, 15)], 6),
-        (g_row.at[pl.ds(0, 15)], 7), (f_got, 8),
+        (c_own.at[0, pl.ds(0, 3)], 4), (c_turn.at[pl.ds(0, 3)], 5), (g_col.at[pl.ds(0, 7)], 6),
+        (g_row.at[pl.ds(0, 15)], 7), (f_got, 8), (c_own.at[1], 18), (count_got, 19), (count_all.at[pl.ds(0, 7)], 20),
     ):
         wait_for(buffer, send_sem, sem)
 
@@ -250,15 +261,18 @@
             pltpu.VMEM((DOCS, tok), F32),
             pltpu.VMEM((QUART * DOCS, span), BF16),
             pltpu.VMEM((4, QUART, 128), BF16),
+            pltpu.VMEM((2, 4, QUART, 128), BF16),
             pltpu.VMEM((4, QUART, 128), BF16),
-            pltpu.VMEM((4, QUART, 128), BF16),
-            pltpu.VMEM((16, DOCS + QUART, COLS), BF16),
+            pltpu.VMEM((8, 2, DOCS, COLS), BF16),
             pltpu.VMEM((16, DOCS, COLS), BF16),
-            pltpu.VMEM((2, 136, COLS), F32),
             pltpu.VMEM((136, COLS), F32),
+            pltpu.VMEM((136, COLS), F32),
+            pltpu.VMEM((8, 128), F32),
+            pltpu.VMEM((8, 128), F32),
+            pltpu.VMEM((8, 8, 128), F32),
             pltpu.SemaphoreType.DMA((3 + HALVES + CHUNKS,)),
-            pltpu.SemaphoreType.DMA((18,)),
-            pltpu.SemaphoreType.DMA((18,)),
+            pltpu.SemaphoreType.DMA((21,)),
+            pltpu.SemaphoreType.DMA((21,)),
         ],
         compiler_params=pltpu.CompilerParams(
             collective_id=0, has_side_effects=True, vmem_limit_bytes=61 * 1024 * 1024

time: 55.9 us -> 51.2 us (0.916)
  Pallas kernels: 54.4 us -> 49.7 us
    pallas_call x1, Pallas kernels: 52.8 us -> 48.1 us  [per_device(): pl.pallas_call(kernel, out_shape=shapes, in_specs=[hbm, hbm, hbm, hbm, hb...]
where the time goes in v4:
time: 51.2 us; the launch traced here: 51 us
  Pallas kernels  49.7 us (97%)
  between operations  1.29 us (3%)
    pallas_call x1, Pallas kernels, per_device(): pl.pallas_call(kernel, out_shape=shapes, in_specs=[hbm, hbm, hbm, hbm, hb...  48.1 us
    pallas_call x1, Pallas kernels, per_device(): pl.pallas_call(hand_over, out_shape=shapes, in_specs=[vmem, vmem], out_sp...  1.59 us

profile of v4, /device:TPU:1, one launch (start us, length us, event | category | flops | bytes accessed | tf_op | source)
XLA Modules:
  0.0 51.0 jit_solution(11273733955681075301)
XLA Ops:
  1.3 48.1 %logra.1 = (bf16[32,256]{1,0:T(8,128)(2,1)}, f32[128,256]{1,0:T(8,128)}) custom-call(bf16[2048,896]{1,0:T(8,128)(2,1)} %acts.1, bf16[2048,256]{1,0:T(8,128)(2,1)} %grads.1, bf16[64,896]{1,0:T(8,128)(2,1)} %bitcast.2, bf16[64,256]{1,0:T(8,128)(2,1)} %bitcast.3, s32[32,2048]{1,0:T(8,128)} %seg.1, s32[1]{0:T(128)S(6)} %copy.8.counts), custom_call_target="tpu_custom_call" | custom-call | flops 1000000000 | bytes 6000000 | tf_op jit(solution)/shard_map/logra/pallas_call | solution.py:240
  49.4 1.6 %hand_over.1 = (bf16[32,256]{1,0:T(8,128)(2,1)}, f32[128,256]{1,0:T(8,128)}) custom-call(bf16[32,256]{1,0:T(8,128)(2,1)} %get-tuple-element.4.doc_in, f32[128,256]{1,0:T(8,128)} %get-tuple-element.5.fis_in), custom_call_target="tpu_custom_call" | custom-call | tf_op jit(solution)/shard_map/hand_over/pallas_call | solution.py:283

commit v5 on v4

--- a/solution.py
+++ b/solution.py
@@ -11,7 +11,7 @@
 RANK = 64
 QUART = 16
 CHUNKS = 4
-HALVES = 2
+PARTS = 4
 DOCS = 32
 COLS = 256
 NT = (((1,), (1,)), ((), ()))
@@ -49,7 +49,7 @@
     on_diagonal = j == k
 
     rows = acts.shape[0] // CHUNKS
-    span = acts.shape[0] // HALVES
+    span = acts.shape[0] // PARTS
 
     def load(src, dst, n):
         copy = pltpu.make_async_copy(src, dst, in_sem.at[n])
@@ -58,10 +58,10 @@
 
     pin_load, pout_load = load(pin, pin_v, 1), load(pout, pout_v, 0)
     grads_load, acts_load = [], []
-    for h in range(HALVES):
-        for n in range(h * CHUNKS // HALVES, (h + 1) * CHUNKS // HALVES):
+    for h in range(PARTS):
+        for n in range(h * CHUNKS // PARTS, (h + 1) * CHUNKS // PARTS):
             part = pl.ds(n * rows, rows)
-            acts_load.append(load(acts.at[part], acts_v.at[part], 3 + HALVES + n))
+            acts_load.append(load(acts.at[part], acts_v.at[part], 3 + PARTS + n))
         part = pl.ds(h * span, span)
         grads_load.append(load(grads.at[part], grads_v.at[part], 3 + h))
     seg_load = load(seg, seg_v, 2)
@@ -89,14 +89,14 @@
         pltpu.make_async_copy(buffer, buffer, sems.at[sem]).wait()
 
     def project(h):
-        for n in range(CHUNKS // HALVES):
+        for n in range(CHUNKS // PARTS):
             part = pl.ds(n * rows, rows)
-            acts_load[h * CHUNKS // HALVES + n].wait()
+            acts_load[h * CHUNKS // PARTS + n].wait()
             product = dot(pin_v[...], acts_v[pl.ds(h * span + n * rows, rows), :], NT)
             x_part[h, :, part] = product
             x_send[h, :, part] = product.astype(BF16)
         grads_load[h].wait()
-        for n in range(CHUNKS // HALVES):
+        for n in range(CHUNKS // PARTS):
             part = pl.ds(n * rows, rows)
             dy_part[h, :, part] = dot(pout_v[...], grads_v[pl.ds(h * span + n * rows, rows), :], NT)
 
@@ -105,16 +105,16 @@
 
     def send_parts(h):
         for d, peer in enumerate(y_peers):
-            remote(x_send.at[h, block((jy + d + 1) % 4)], x_got.at[h, d], 10 + h, peer).start()
+            remote(x_send.at[h, block((jy + d + 1) % 4)], x_got.at[h, d], 22 + h, peer).start()
         for d, peer in enumerate(x_peers):
-            remote(dy_part.at[h, block((jx + d + 1) % 4)], dy_got.at[h, d], 12 + h, peer).start()
+            remote(dy_part.at[h, block((jx + d + 1) % 4)], dy_got.at[h, d], 26 + h, peer).start()
 
     pout_load.wait()
     pin_load.wait()
     project(0)
     pl.semaphore_wait(barrier, jnp.where(on_diagonal, 33, 35))
     send_parts(0)
-    for h in range(1, HALVES):
+    for h in range(1, PARTS):
         project(h)
         send_parts(h)
 
@@ -124,18 +124,18 @@
     count_own[...] = jnp.full(count_own.shape, jnp.sum(live), F32)
     remote(count_own, count_got, 19, across[0]).start()
 
-    for h in range(HALVES):
-        wait_for(dy_got.at[h], recv_sem, 12 + h)
+    for h in range(PARTS):
+        wait_for(dy_got.at[h], recv_sem, 26 + h)
         dy_sum = dy_part[h, block(jx), :] + dy_got[h, 0] + dy_got[h, 1] + dy_got[h, 2]
         dy_all[h] = dy_sum
         dy_send2[h] = dy_sum.astype(BF16)
         for d, peer in enumerate(y_peers):
-            remote(dy_send2.at[h], dy_got2.at[h, d], 14 + h, peer).start()
-        wait_for(x_got.at[h], recv_sem, 10 + h)
+            remote(dy_send2.at[h], dy_got2.at[h, d], 30 + h, peer).start()
+        wait_for(x_got.at[h], recv_sem, 22 + h)
         got = [x_got[h, d].astype(F32) for d in range(3)]
         x_send2[h] = x_part[h, block(jy), :] + got[0] + got[1] + got[2]
         for d, peer in enumerate(x_peers):
-            remote(x_send2.at[h], x_got2.at[h, d], 16 + h, peer).start()
+            remote(x_send2.at[h], x_got2.at[h, d], 34 + h, peer).start()
 
     wait_for(count_got, recv_sem, 19)
     count_all[z] = count_own[...] + count_got[...]
@@ -143,14 +143,14 @@
         remote(count_all.at[z], count_all.at[z], 20, peer).start()
 
     both = jnp.zeros((2 * QUART, QUART * DOCS), F32)
-    for h in range(HALVES):
-        wait_for(dy_got2.at[h], recv_sem, 14 + h)
+    for h in range(PARTS):
+        wait_for(dy_got2.at[h], recv_sem, 30 + h)
         got = [dy_got2[h, d].astype(F32) for d in range(3)]
         dy_full = dy_all[h] + got[0] + got[1] + got[2]
         mask = live_v[:, h * span : (h + 1) * span]
         for a in range(QUART):
             wide[a * DOCS : (a + 1) * DOCS, :] = (mask * dy_full[a : a + 1, :]).astype(BF16)
-        wait_for(x_got2.at[h], recv_sem, 16 + h)
+        wait_for(x_got2.at[h], recv_sem, 34 + h)
         x_full = x_send2[h] + x_got2[h, 0] + x_got2[h, 1] + x_got2[h, 2]
         x_high = x_full.astype(BF16)
         x_low = (x_full - x_high.astype(F32)).astype(BF16)
@@ -213,8 +213,8 @@
     wait_for(f_got, recv_sem, 8)
     fis_out[...] = (mine + f_got[:128]) / (f_got[128:129, :] + live_tokens)
 
-    for h in range(HALVES):
-        for buffer, sem in ((x_got, 10), (dy_got, 12), (dy_got2, 14), (x_got2, 16)):
+    for h in range(PARTS):
+        for buffer, sem in ((x_got, 22), (dy_got, 26), (dy_got2, 30), (x_got2, 34)):
             wait_for(buffer.at[h], send_sem, sem + h)
     for buffer, sem in (
         (c_own.at[0, pl.ds(0, 3)], 4), (c_turn.at[pl.ds(0, 3)], 5), (g_col.at[pl.ds(0, 7)], 6),
@@ -234,12 +234,12 @@
 
 def per_device(acts, grads, pin, pout, seg, counts):
     tok, hidden = acts.shape
-    width, span = grads.shape[1], tok // HALVES
+    width, span = grads.shape[1], tok // PARTS
     vmem, hbm, smem = (pl.BlockSpec(memory_space=m) for m in (pltpu.VMEM, pltpu.HBM, pltpu.SMEM))
     shapes = (jax.ShapeDtypeStruct((DOCS, COLS), BF16), jax.ShapeDtypeStruct((128, COLS), F32))
     results = pl.pallas_call(
         kernel,
-        out_shape=shapes,
+        out_shape=(pltpu.VMEM((DOCS, COLS), BF16), pltpu.VMEM((128, COLS), F32)),
         in_specs=[hbm, hbm, hbm, hbm, hbm, smem],
         out_specs=(vmem, vmem),
         scratch_shapes=[
@@ -248,16 +248,16 @@
             pltpu.VMEM((RANK, hidden), BF16),
             pltpu.VMEM((RANK, width), BF16),
             pltpu.VMEM((DOCS, tok), jnp.int32),
-            pltpu.VMEM((HALVES, RANK, span), F32),
-            pltpu.VMEM((HALVES, RANK, span), F32),
-            pltpu.VMEM((HALVES, RANK, span), BF16),
-            pltpu.VMEM((HALVES, 3, QUART, span), F32),
-            pltpu.VMEM((HALVES, 3, QUART, span), BF16),
-            pltpu.VMEM((HALVES, QUART, span), BF16),
-            pltpu.VMEM((HALVES, QUART, span), F32),
-            pltpu.VMEM((HALVES, 3, QUART, span), BF16),
-            pltpu.VMEM((HALVES, 3, QUART, span), F32),
-            pltpu.VMEM((HALVES, QUART, span), F32),
+            pltpu.VMEM((PARTS, RANK, span), F32),
+            pltpu.VMEM((PARTS, RANK, span), F32),
+            pltpu.VMEM((PARTS, RANK, span), BF16),
+            pltpu.VMEM((PARTS, 3, QUART, span), F32),
+            pltpu.VMEM((PARTS, 3, QUART, span), BF16),
+            pltpu.VMEM((PARTS, QUART, span), BF16),
+            pltpu.VMEM((PARTS, QUART, span), F32),
+            pltpu.VMEM((PARTS, 3, QUART, span), BF16),
+            pltpu.VMEM((PARTS, 3, QUART, span), F32),
+            pltpu.VMEM((PARTS, QUART, span), F32),
             pltpu.VMEM((DOCS, tok), F32),
             pltpu.VMEM((QUART * DOCS, span), BF16),
             pltpu.VMEM((4, QUART, 128), BF16),
@@ -270,12 +270,12 @@
             pltpu.VMEM((8, 128), F32),
             pltpu.VMEM((8, 128), F32),
             pltpu.VMEM((8, 8, 128), F32),
-            pltpu.SemaphoreType.DMA((3 + HALVES + CHUNKS,)),
-            pltpu.SemaphoreType.DMA((21,)),
-            pltpu.SemaphoreType.DMA((21,)),
+            pltpu.SemaphoreType.DMA((3 + PARTS + CHUNKS,)),
+            pltpu.SemaphoreType.DMA((40,)),
+            pltpu.SemaphoreType.DMA((40,)),
         ],
         compiler_params=pltpu.CompilerParams(
-            collective_id=0, has_side_effects=True, vmem_limit_bytes=61 * 1024 * 1024
+            collective_id=0, has_side_effects=True, vmem_limit_bytes=60 * 1024 * 1024
         ),
         cost_estimate=pl.CostEstimate(flops=10**9, bytes_accessed=6 * 10**6, transcendentals=0),
         name="logra",
@@ -285,7 +285,7 @@
         out_shape=shapes,
         in_specs=[vmem, vmem],
         out_specs=(vmem, vmem),
-        compiler_params=pltpu.CompilerParams(vmem_limit_bytes=61 * 1024 * 1024),
+        compiler_params=pltpu.CompilerParams(vmem_limit_bytes=4 * 1024 * 1024),
         name="hand_over",
     )(*results)
 

time: 51.2 us -> 48.8 us (0.953)
  Pallas kernels: 49.7 us -> 47.4 us
    pallas_call x1, Pallas kernels: 48.1 us -> 46.7 us  [per_device(): pl.pallas_call(kernel, out_shape=(pltpu.VMEM((DOCS, COLS), BF16), pltpu.V...]
    pallas_call x1, Pallas kernels: 1.59 us -> 0.67 us  [per_device(): pl.pallas_call(hand_over, out_shape=shapes, in_specs=[vmem, vmem], out_sp...]
where the time goes in v5:
time: 48.8 us; the launch traced here: 48.7 us
  Pallas kernels  47.4 us (97%)
  between operations  1.29 us (3%)
    pallas_call x1, Pallas kernels, per_device(): pl.pallas_call(kernel, out_shape=(pltpu.VMEM((DOCS, COLS), BF16), pltpu.V...  46.7 us

profile of v5, /device:TPU:1, one launch (start us, length us, event | category | flops | bytes accessed | tf_op | source)
XLA Modules:
  0.0 48.7 jit_solution(4833449095331322872)
XLA Ops:
  1.3 46.7 %logra.1 = (bf16[32,256]{1,0:T(8,128)(2,1)S(1)}, f32[128,256]{1,0:T(8,128)S(1)}) custom-call(bf16[2048,896]{1,0:T(8,128)(2,1)} %acts.1, bf16[2048,256]{1,0:T(8,128)(2,1)} %grads.1, bf16[64,896]{1,0:T(8,128)(2,1)} %bitcast.2, bf16[64,256]{1,0:T(8,128)(2,1)} %bitcast.3, s32[32,2048]{1,0:T(8,128)} %seg.1, s32[1]{0:T(128)S(6)} %copy.8.counts), custom_call_target="tpu_custom_call" | custom-call | flops 1000000000 | bytes 6000000 | tf_op jit(solution)/shard_map/logra/pallas_call | solution.py:240
  48.0 0.7 %hand_over.1 = (bf16[32,256]{1,0:T(8,128)(2,1)}, f32[128,256]{1,0:T(8,128)}) custom-call(bf16[32,256]{1,0:T(8,128)(2,1)S(1)} %get-tuple-element.4.doc_in, f32[128,256]{1,0:T(8,128)S(1)} %get-tuple-element.5.fis_in), custom_call_target="tpu_custom_call" | custom-call | tf_op jit(solution)/shard_map/hand_over/pallas_call | solution.py:283

commit v6 on v5

--- a/solution.py
+++ b/solution.py
@@ -58,13 +58,15 @@
 
     pin_load, pout_load = load(pin, pin_v, 1), load(pout, pout_v, 0)
     grads_load, acts_load = [], []
-    for h in range(PARTS):
+
+    def load_part(h):
         for n in range(h * CHUNKS // PARTS, (h + 1) * CHUNKS // PARTS):
             part = pl.ds(n * rows, rows)
             acts_load.append(load(acts.at[part], acts_v.at[part], 3 + PARTS + n))
         part = pl.ds(h * span, span)
         grads_load.append(load(grads.at[part], grads_v.at[part], 3 + h))
-    seg_load = load(seg, seg_v, 2)
+
+    load_part(0)
 
     barrier = pltpu.get_barrier_semaphore()
 
@@ -78,6 +80,10 @@
     def _():
         greet(turn_to[0])
         greet(turn_from[0])
+
+    for h in range(1, PARTS):
+        load_part(h)
+    seg_load = load(seg, seg_v, 2)
 
     def remote(src, dst, sem, peer):
         return pltpu.make_async_remote_copy(
@@ -104,7 +110,7 @@
         return pl.ds(pl.multiple_of(index * QUART, QUART), QUART)
 
     def send_parts(h):
-        for d, peer in enumerate(y_peers):
+        for d, peer in ((1, y_peers[1]), (2, y_peers[2]), (0, y_peers[0])):
             remote(x_send.at[h, block((jy + d + 1) % 4)], x_got.at[h, d], 22 + h, peer).start()
         for d, peer in enumerate(x_peers):
             remote(dy_part.at[h, block((jx + d + 1) % 4)], dy_got.at[h, d], 26 + h, peer).start()
@@ -129,7 +135,7 @@
         dy_sum = dy_part[h, block(jx), :] + dy_got[h, 0] + dy_got[h, 1] + dy_got[h, 2]
         dy_all[h] = dy_sum
         dy_send2[h] = dy_sum.astype(BF16)
-        for d, peer in enumerate(y_peers):
+        for d, peer in ((1, y_peers[1]), (2, y_peers[2]), (0, y_peers[0])):
             remote(dy_send2.at[h], dy_got2.at[h, d], 30 + h, peer).start()
         wait_for(x_got.at[h], recv_sem, 22 + h)
         got = [x_got[h, d].astype(F32) for d in range(3)]

time: 48.8 us -> 48.3 us (0.990)
  Pallas kernels: 47.4 us -> 46.9 us
where the time goes in v6:
time: 48.3 us; the launch traced here: 48.2 us
  Pallas kernels  46.9 us (97%)
  between operations  1.29 us (3%)
    pallas_call x1, Pallas kernels, per_device(): pl.pallas_call(kernel, out_shape=(pltpu.VMEM((DOCS, COLS), BF16), pltpu.V...  46.3 us

profile of v6, /device:TPU:1, one launch (start us, length us, event | category | flops | bytes accessed | tf_op | source)
XLA Modules:
  0.0 48.2 jit_solution(5434145570952382873)
XLA Ops:
  1.3 46.3 %logra.1 = (bf16[32,256]{1,0:T(8,128)(2,1)S(1)}, f32[128,256]{1,0:T(8,128)S(1)}) custom-call(bf16[2048,896]{1,0:T(8,128)(2,1)} %acts.1, bf16[2048,256]{1,0:T(8,128)(2,1)} %grads.1, bf16[64,896]{1,0:T(8,128)(2,1)} %bitcast.2, bf16[64,256]{1,0:T(8,128)(2,1)} %bitcast.3, s32[32,2048]{1,0:T(8,128)} %seg.1, s32[1]{0:T(128)S(6)} %copy.8.counts), custom_call_target="tpu_custom_call" | custom-call | flops 1000000000 | bytes 6000000 | tf_op jit(solution)/shard_map/logra/pallas_call | solution.py:246
  47.5 0.7 %hand_over.1 = (bf16[32,256]{1,0:T(8,128)(2,1)}, f32[128,256]{1,0:T(8,128)}) custom-call(bf16[32,256]{1,0:T(8,128)(2,1)S(1)} %get-tuple-element.4.doc_in, f32[128,256]{1,0:T(8,128)S(1)} %get-tuple-element.5.fis_in), custom_call_target="tpu_custom_call" | custom-call | tf_op jit(solution)/shard_map/hand_over/pallas_call | solution.py:289

commit v7 on v6

--- a/solution.py
+++ b/solution.py
@@ -112,7 +112,7 @@
     def send_parts(h):
         for d, peer in ((1, y_peers[1]), (2, y_peers[2]), (0, y_peers[0])):
             remote(x_send.at[h, block((jy + d + 1) % 4)], x_got.at[h, d], 22 + h, peer).start()
-        for d, peer in enumerate(x_peers):
+        for d, peer in ((1, x_peers[1]), (0, x_peers[0]), (2, x_peers[2])):
             remote(dy_part.at[h, block((jx + d + 1) % 4)], dy_got.at[h, d], 26 + h, peer).start()
 
     pout_load.wait()
@@ -140,7 +140,7 @@
         wait_for(x_got.at[h], recv_sem, 22 + h)
         got = [x_got[h, d].astype(F32) for d in range(3)]
         x_send2[h] = x_part[h, block(jy), :] + got[0] + got[1] + got[2]
-        for d, peer in enumerate(x_peers):
+        for d, peer in ((1, x_peers[1]), (0, x_peers[0]), (2, x_peers[2])):
             remote(x_send2.at[h], x_got2.at[h, d], 34 + h, peer).start()
 
     wait_for(count_got, recv_sem, 19)

time: 48.3 us -> 48.1 us (level)
  no operation moved by 1% of the time
where the time goes in v7:
time: 48.1 us; the launch traced here: 48 us
  Pallas kernels  46.7 us (97%)
  between operations  1.29 us (3%)
    pallas_call x1, Pallas kernels, per_device(): pl.pallas_call(kernel, out_shape=(pltpu.VMEM((DOCS, COLS), BF16), pltpu.V...  46 us

profile of v7, /device:TPU:1, one launch (start us, length us, event | category | flops | bytes accessed | tf_op | source)
XLA Modules:
  0.0 48.0 jit_solution(9449059657264677869)
XLA Ops:
  1.3 46.0 %logra.1 = (bf16[32,256]{1,0:T(8,128)(2,1)S(1)}, f32[128,256]{1,0:T(8,128)S(1)}) custom-call(bf16[2048,896]{1,0:T(8,128)(2,1)} %acts.1, bf16[2048,256]{1,0:T(8,128)(2,1)} %grads.1, bf16[64,896]{1,0:T(8,128)(2,1)} %bitcast.2, bf16[64,256]{1,0:T(8,128)(2,1)} %bitcast.3, s32[32,2048]{1,0:T(8,128)} %seg.1, s32[1]{0:T(128)S(6)} %copy.8.counts), custom_call_target="tpu_custom_call" | custom-call | flops 1000000000 | bytes 6000000 | tf_op jit(solution)/shard_map/logra/pallas_call | solution.py:246
  47.3 0.7 %hand_over.1 = (bf16[32,256]{1,0:T(8,128)(2,1)}, f32[128,256]{1,0:T(8,128)}) custom-call(bf16[32,256]{1,0:T(8,128)(2,1)S(1)} %get-tuple-element.4.doc_in, f32[128,256]{1,0:T(8,128)S(1)} %get-tuple-element.5.fis_in), custom_call_target="tpu_custom_call" | custom-call | tf_op jit(solution)/shard_map/hand_over/pallas_call | solution.py:289
